TPU v7x, 32 devices: a whole 2x2x4 slice. The times are simulated.
32 devices in a mesh: groups: 2 (over y), dp: 4 (over z), mp: 4 (over x, core).
Axes of the slice: x: 2, y: 2, z: 4, core: 2. Of those that a mesh axis runs over, the one named last changes fastest.
Arguments:
- embeddings: bfloat16 [16384, 1024], P(('groups', 'dp')), parts along dimension 0, may hold values from -60 to 60
- rotation: bfloat16 [1024, 1024], P(None, 'mp'), may hold values from -0.1875 to 0.1875
- codes: int32 [2, 16384, 16], P(None, ('groups', 'dp'), 'mp'), parts along dimension 1, may hold values from 0 to 255
Outputs:
- centroids: bfloat16 [512, 1024], P('groups', 'mp'), parts along dimension 0
- new_rotation: float32 [2048, 1024], P(('groups', 'dp'), 'mp'), parts along dimension 0
- rotated: bfloat16 [16384, 1024], P(('groups', 'dp'), 'mp'), parts along dimension 0
There are 2 independent parts, one for each index of `groups`. A program takes and returns all parts, laid end to end along the dimension named above; an argument that names none is the same for every part. Nothing has to cross between parts.
All inputs are finite; a program needn't handle non-finite values.
Results may differ from a plain program's by a relative error of at most 0.014.
The roundings to bfloat16 on the way count: a program that leaves them out, or rounds other values in their place, can miss the bound.
Values may be sent and summed in bfloat16 or wider, within the bound.
A program may use at most 64 MiB of HBM per device.

v0:
```python
import jax
import jax.numpy as jnp
from jax import lax
from jax.sharding import PartitionSpec as P

SUB = 64
K = 256
ALTS = 2
NS_STEPS = 5


coef_one = 3.4445
coef_two = -4.775
coef_three = 2.0315


def body(embeddings, rotation, codes):
    col_count = rotation.shape[1]
    local_subs = col_count // SUB
    row_count = embeddings.shape[0]
    levels = jnp.arange(K, dtype=jnp.int32)
    highest = lax.Precision.HIGHEST
    rot_cols = rotation
    centres = jnp.zeros((K, local_subs, SUB), jnp.bfloat16)
    polar = jnp.zeros((1, 1), jnp.float32)
    for alternation in range(ALTS):
        turned = jnp.dot(embeddings, rot_cols, preferred_element_type=jnp.float32).astype(
            jnp.bfloat16
        )
        selector = (codes[alternation][:, :, None] == levels).astype(jnp.bfloat16)
        pieces = turned.reshape(row_count, local_subs, SUB)
        class_sum = jnp.einsum("rlk,rls->kls", selector, pieces, preferred_element_type=jnp.float32)
        class_count = jnp.sum(selector, axis=0, dtype=jnp.float32).T
        class_sum, class_count = lax.psum((class_sum, class_count), "dp")
        centres = (class_sum / (class_count[:, :, None] + 1.0)).astype(jnp.bfloat16)
        picked = jnp.einsum("rlk,kls->rls", selector, centres, preferred_element_type=jnp.float32)
        picked = picked.astype(jnp.bfloat16).reshape(row_count, col_count)
        cross_part = lax.dot_general(
            embeddings, picked, (((0,), (0,)), ((), ())), preferred_element_type=jnp.float32
        )
        cross_tile = lax.psum_scatter(cross_part, "dp", scatter_dimension=0, tiled=True)
        square_sum = lax.psum(jnp.sum(cross_tile * cross_tile), ("dp", "mp"))
        polar = cross_tile / (jnp.sqrt(square_sum) + 1e-06)
        for iterate in range(NS_STEPS):
            polar_band = lax.all_gather(polar, "mp", axis=1, tiled=True)
            narrow_band = lax.all_to_all(polar_band, "dp", split_axis=1, concat_axis=0, tiled=True)
            col_block = lax.all_gather(polar, "dp", axis=0, tiled=True)
            gram_piece = lax.dot_general(
                narrow_band,
                col_block,
                (((0,), (0,)), ((), ())),
                precision=highest,
                preferred_element_type=jnp.float32,
            )
            gram_cols = lax.all_gather(gram_piece, "dp", axis=0, tiled=True)
            first_prod = jnp.dot(
                polar_band, gram_cols, precision=highest, preferred_element_type=jnp.float32
            )
            first_band = lax.all_gather(first_prod, "mp", axis=1, tiled=True)
            second_prod = jnp.dot(
                first_band, gram_cols, precision=highest, preferred_element_type=jnp.float32
            )
            polar = coef_one * polar + coef_two * first_prod + coef_three * second_prod
        rot_cols = lax.all_gather(polar.astype(jnp.bfloat16), "dp", axis=0, tiled=True)
    rotated = jnp.dot(embeddings, rot_cols, preferred_element_type=jnp.float32).astype(jnp.bfloat16)
    return (centres.reshape(K, col_count), polar, rotated)


def solution(mesh):
    placed = (P(("groups", "dp"), None), P(None, "mp"), P(None, ("groups", "dp"), "mp"))
    return jax.shard_map(
        body,
        mesh=mesh,
        in_specs=placed,
        out_specs=(P("groups", "mp"), P(("groups", "dp"), "mp"), P(("groups", "dp"), "mp")),
        check_vma=False,
    )
```

profile of v0, /device:TPU:0, one launch (start us, length us, event | category | flops | bytes accessed | tf_op | source)
XLA Modules:
  0.0 1486.1 jit_solution(16368945491137155537)
XLA Ops:
  17.6 13.7 all-reduce
  31.3 21.7 %all-reduce.4.cloned.1.call-done = f32[256,4,64]{0,2,1:T(8,128)} async-done(((f32[256,4,64]{0,2,1:T(8,128)}), f32[256,4,64]{0,2,1:T(8,128)}) %all-reduce.4.cloned.1.call-update) | async-done | bytes 262160 | tf_op jit(solution)/shard_map/psum | solution.py:34
  60.2 27.0 %reduce-scatter.3.cloned.1.call-done = f32[256,256]{0,1:T(8,128)} async-done(((f32[1024,256]{0,1:T(8,128)}), f32[256,256]{0,1:T(8,128)}) %reduce-scatter.3.cloned.1.call-update) | async-done | bytes 262160 | tf_op jit(solution)/shard_map/reduce_scatter | solution.py:41
  88.9 31.1 %psum.44 = f32[]{:T(128)} all-reduce(f32[]{:T(128)} %multiply_reduce_fusion.1), channel_id=1, replica_groups=mesh['groups'=2,'dp'=4,'mp'=4] {'dp','mp'}, use_global_device_ids=true, to_apply=%region_5.0 | all-reduce | flops 1 | bytes 8 | tf_op jit(solution)/shard_map/psum | solution.py:42
  143.8 41.5 %all-gather.43.cloned.1.call-done = f32[1024,256]{0,1:T(8,128)} async-done(((f32[256,256]{0,1:T(8,128)}), f32[1024,256]{0,1:T(8,128)}) %all-gather.43.cloned.1.call-update) | async-done | bytes 1048592 | tf_op jit(solution)/shard_map/all_gather | solution.py:47
  190.6 26.3 %all-gather.45.cloned.1.call-done = f32[1024,256]{1,0:T(8,128)} async-done(((f32[256,256]{1,0:T(8,128)}), f32[1024,256]{1,0:T(8,128)}) %all-gather.45.cloned.1.call-update) | async-done | bytes 1048592 | tf_op jit(solution)/shard_map/all_gather | solution.py:55
  221.8 15.2 %all-gather.47.cloned.1.call-done = f32[256,1024]{1,0:T(8,128)} async-done(((f32[256,256]{1,0:T(8,128)}), f32[256,1024]{1,0:T(8,128)}) %all-gather.47.cloned.1.call-update) | async-done | bytes 1048592 | tf_op jit(solution)/shard_map/all_gather | solution.py:59
  241.9 16.1 %all-gather.49.cloned.1.call-done = f32[256,1024]{0,1:T(8,128)} async-done(((f32[256,256]{0,1:T(8,128)}), f32[256,1024]{0,1:T(8,128)}) %all-gather.49.cloned.1.call-update) | async-done | bytes 1048592 | tf_op jit(solution)/shard_map/all_gather | solution.py:45
  265.5 41.4 %all-gather.51.cloned.1.call-done = f32[1024,256]{0,1:T(8,128)} async-done(((f32[256,256]{0,1:T(8,128)}), f32[1024,256]{0,1:T(8,128)}) %all-gather.51.cloned.1.call-update) | async-done | bytes 1048592 | tf_op jit(solution)/shard_map/all_gather | solution.py:47
  312.2 26.4 %all-gather.53.cloned.1.call-done = f32[1024,256]{1,0:T(8,128)} async-done(((f32[256,256]{1,0:T(8,128)}), f32[1024,256]{1,0:T(8,128)}) %all-gather.53.cloned.1.call-update) | async-done | bytes 1048592 | tf_op jit(solution)/shard_map/all_gather | solution.py:55
  343.4 15.2 %all-gather.55.cloned.1.call-done = f32[256,1024]{1,0:T(8,128)} async-done(((f32[256,256]{1,0:T(8,128)}), f32[256,1024]{1,0:T(8,128)}) %all-gather.55.cloned.1.call-update) | async-done | bytes 1048592 | tf_op jit(solution)/shard_map/all_gather | solution.py:59
  363.3 16.3 %all-gather.57.cloned.1.call-done = f32[256,1024]{0,1:T(8,128)} async-done(((f32[256,256]{0,1:T(8,128)}), f32[256,1024]{0,1:T(8,128)}) %all-gather.57.cloned.1.call-update) | async-done | bytes 1048592 | tf_op jit(solution)/shard_map/all_gather | solution.py:45
  387.0 41.5 %all-gather.59.cloned.1.call-done = f32[1024,256]{0,1:T(8,128)} async-done(((f32[256,256]{0,1:T(8,128)}), f32[1024,256]{0,1:T(8,128)}) %all-gather.59.cloned.1.call-update) | async-done | bytes 1048592 | tf_op jit(solution)/shard_map/all_gather | solution.py:47
  433.8 26.3 %all-gather.61.cloned.1.call-done = f32[1024,256]{1,0:T(8,128)} async-done(((f32[256,256]{1,0:T(8,128)}), f32[1024,256]{1,0:T(8,128)}) %all-gather.61.cloned.1.call-update) | async-done | bytes 1048592 | tf_op jit(solution)/shard_map/all_gather | solution.py:55
  465.0 15.2 %all-gather.63.cloned.1.call-done = f32[256,1024]{1,0:T(8,128)} async-done(((f32[256,256]{1,0:T(8,128)}), f32[256,1024]{1,0:T(8,128)}) %all-gather.63.cloned.1.call-update) | async-done | bytes 1048592 | tf_op jit(solution)/shard_map/all_gather | solution.py:59
  484.9 16.3 %all-gather.65.cloned.1.call-done = f32[256,1024]{0,1:T(8,128)} async-done(((f32[256,256]{0,1:T(8,128)}), f32[256,1024]{0,1:T(8,128)}) %all-gather.65.cloned.1.call-update) | async-done | bytes 1048592 | tf_op jit(solution)/shard_map/all_gather | solution.py:45
  508.5 41.5 %all-gather.67.cloned.1.call-done = f32[1024,256]{0,1:T(8,128)} async-done(((f32[256,256]{0,1:T(8,128)}), f32[1024,256]{0,1:T(8,128)}) %all-gather.67.cloned.1.call-update) | async-done | bytes 1048592 | tf_op jit(solution)/shard_map/all_gather | solution.py:47
  555.3 26.3 %all-gather.69.cloned.1.call-done = f32[1024,256]{1,0:T(8,128)} async-done(((f32[256,256]{1,0:T(8,128)}), f32[1024,256]{1,0:T(8,128)}) %all-gather.69.cloned.1.call-update) | async-done | bytes 1048592 | tf_op jit(solution)/shard_map/all_gather | solution.py:55
  586.5 15.2 %all-gather.71.cloned.1.call-done = f32[256,1024]{1,0:T(8,128)} async-done(((f32[256,256]{1,0:T(8,128)}), f32[256,1024]{1,0:T(8,128)}) %all-gather.71.cloned.1.call-update) | async-done | bytes 1048592 | tf_op jit(solution)/shard_map/all_gather | solution.py:59
  606.4 16.3 %all-gather.73.cloned.1.call-done = f32[256,1024]{0,1:T(8,128)} async-done(((f32[256,256]{0,1:T(8,128)}), f32[256,1024]{0,1:T(8,128)}) %all-gather.73.cloned.1.call-update) | async-done | bytes 1048592 | tf_op jit(solution)/shard_map/all_gather | solution.py:45
  630.1 41.5 %all-gather.75.cloned.1.call-done = f32[1024,256]{0,1:T(8,128)} async-done(((f32[256,256]{0,1:T(8,128)}), f32[1024,256]{0,1:T(8,128)}) %all-gather.75.cloned.1.call-update) | async-done | bytes 1048592 | tf_op jit(solution)/shard_map/all_gather | solution.py:47
  676.9 26.3 %all-gather.77.cloned.1.call-done = f32[1024,256]{1,0:T(8,128)} async-done(((f32[256,256]{1,0:T(8,128)}), f32[1024,256]{1,0:T(8,128)}) %all-gather.77.cloned.1.call-update) | async-done | bytes 1048592 | tf_op jit(solution)/shard_map/all_gather | solution.py:55
  708.5 14.8 all-gather.79.cloned.1.call-done
  726.7 16.1 %all_gather.146 = bf16[1024,256]{0,1:T(8,128)(2,1)S(1)} all-gather(bf16[256,256]{0,1:T(8,128)(2,1)S(1)} %fusion.25), channel_id=1, replica_groups=mesh['groups'=2,'dp'=4,'mp'=4] {'dp'}, dimensions={0}, use_global_device_ids=true | all-gather | bytes 655360 | tf_op jit(solution)/shard_map/all_gather | solution.py:64
  749.2 35.8 %all-reduce.6.cloned.1.call-done = f32[256,4,64]{0,2,1:T(8,128)} async-done(((f32[256,4,64]{0,2,1:T(8,128)}), f32[256,4,64]{0,2,1:T(8,128)}) %all-reduce.6.cloned.1.call-update) | async-done | bytes 262160 | tf_op jit(solution)/shard_map/psum | solution.py:34
  790.7 27.0 %reduce-scatter.5.cloned.1.call-done = f32[256,256]{0,1:T(8,128)} async-done(((f32[1024,256]{0,1:T(8,128)}), f32[256,256]{0,1:T(8,128)}) %reduce-scatter.5.cloned.1.call-update) | async-done | bytes 262160 | tf_op jit(solution)/shard_map/reduce_scatter | solution.py:41
  819.3 31.1 %psum.47 = f32[]{:T(128)} all-reduce(f32[]{:T(128)} %multiply_reduce_fusion), channel_id=1, replica_groups=mesh['groups'=2,'dp'=4,'mp'=4] {'dp','mp'}, use_global_device_ids=true, to_apply=%region_11.0 | all-reduce | flops 1 | bytes 8 | tf_op jit(solution)/shard_map/psum | solution.py:42
  853.4 13.5 all-gather.81.cloned.1.call-done
  874.3 41.5 %all-gather.83.cloned.1.call-done = f32[1024,256]{0,1:T(8,128)} async-done(((f32[256,256]{0,1:T(8,128)}), f32[1024,256]{0,1:T(8,128)}) %all-gather.83.cloned.1.call-update) | async-done | bytes 1048592 | tf_op jit(solution)/shard_map/all_gather | solution.py:47
  921.1 26.3 %all-gather.85.cloned.1.call-done = f32[1024,256]{1,0:T(8,128)} async-done(((f32[256,256]{1,0:T(8,128)}), f32[1024,256]{1,0:T(8,128)}) %all-gather.85.cloned.1.call-update) | async-done | bytes 1048592 | tf_op jit(solution)/shard_map/all_gather | solution.py:55
  952.3 15.2 %all-gather.87.cloned.1.call-done = f32[256,1024]{1,0:T(8,128)} async-done(((f32[256,256]{1,0:T(8,128)}), f32[256,1024]{1,0:T(8,128)}) %all-gather.87.cloned.1.call-update) | async-done | bytes 1048592 | tf_op jit(solution)/shard_map/all_gather | solution.py:59
  972.2 16.3 %all-gather.89.cloned.1.call-done = f32[256,1024]{0,1:T(8,128)} async-done(((f32[256,256]{0,1:T(8,128)}), f32[256,1024]{0,1:T(8,128)}) %all-gather.89.cloned.1.call-update) | async-done | bytes 1048592 | tf_op jit(solution)/shard_map/all_gather | solution.py:45
  995.9 41.5 %all-gather.91.cloned.1.call-done = f32[1024,256]{0,1:T(8,128)} async-done(((f32[256,256]{0,1:T(8,128)}), f32[1024,256]{0,1:T(8,128)}) %all-gather.91.cloned.1.call-update) | async-done | bytes 1048592 | tf_op jit(solution)/shard_map/all_gather | solution.py:47
  1042.7 26.3 %all-gather.93.cloned.1.call-done = f32[1024,256]{1,0:T(8,128)} async-done(((f32[256,256]{1,0:T(8,128)}), f32[1024,256]{1,0:T(8,128)}) %all-gather.93.cloned.1.call-update) | async-done | bytes 1048592 | tf_op jit(solution)/shard_map/all_gather | solution.py:55
  1073.9 15.2 %all-gather.95.cloned.1.call-done = f32[256,1024]{1,0:T(8,128)} async-done(((f32[256,256]{1,0:T(8,128)}), f32[256,1024]{1,0:T(8,128)}) %all-gather.95.cloned.1.call-update) | async-done | bytes 1048592 | tf_op jit(solution)/shard_map/all_gather | solution.py:59
  1093.9 16.1 %all-gather.97.cloned.1.call-done = f32[256,1024]{0,1:T(8,128)} async-done(((f32[256,256]{0,1:T(8,128)}), f32[256,1024]{0,1:T(8,128)}) %all-gather.97.cloned.1.call-update) | async-done | bytes 1048592 | tf_op jit(solution)/shard_map/all_gather | solution.py:45
  1117.4 41.5 %all-gather.99.cloned.1.call-done = f32[1024,256]{0,1:T(8,128)} async-done(((f32[256,256]{0,1:T(8,128)}), f32[1024,256]{0,1:T(8,128)}) %all-gather.99.cloned.1.call-update) | async-done | bytes 1048592 | tf_op jit(solution)/shard_map/all_gather | solution.py:47
  1164.2 26.4 %all-gather.101.cloned.1.call-done = f32[1024,256]{1,0:T(8,128)} async-done(((f32[256,256]{1,0:T(8,128)}), f32[1024,256]{1,0:T(8,128)}) %all-gather.101.cloned.1.call-update) | async-done | bytes 1048592 | tf_op jit(solution)/shard_map/all_gather | solution.py:55
  1195.7 15.0 %all-gather.103.cloned.1.call-done = f32[256,1024]{1,0:T(8,128)} async-done(((f32[256,256]{1,0:T(8,128)}), f32[256,1024]{1,0:T(8,128)}) %all-gather.103.cloned.1.call-update) | async-done | bytes 1048592 | tf_op jit(solution)/shard_map/all_gather | solution.py:59
  1215.6 16.1 %all-gather.105.cloned.1.call-done = f32[256,1024]{0,1:T(8,128)} async-done(((f32[256,256]{0,1:T(8,128)}), f32[256,1024]{0,1:T(8,128)}) %all-gather.105.cloned.1.call-update) | async-done | bytes 1048592 | tf_op jit(solution)/shard_map/all_gather | solution.py:45
  1239.0 41.5 %all-gather.107.cloned.1.call-done = f32[1024,256]{0,1:T(8,128)} async-done(((f32[256,256]{0,1:T(8,128)}), f32[1024,256]{0,1:T(8,128)}) %all-gather.107.cloned.1.call-update) | async-done | bytes 1048592 | tf_op jit(solution)/shard_map/all_gather | solution.py:47
  1285.8 26.4 %all-gather.109.cloned.1.call-done = f32[1024,256]{1,0:T(8,128)} async-done(((f32[256,256]{1,0:T(8,128)}), f32[1024,256]{1,0:T(8,128)}) %all-gather.109.cloned.1.call-update) | async-done | bytes 1048592 | tf_op jit(solution)/shard_map/all_gather | solution.py:55
  1317.1 15.2 %all-gather.111.cloned.1.call-done = f32[256,1024]{1,0:T(8,128)} async-done(((f32[256,256]{1,0:T(8,128)}), f32[256,1024]{1,0:T(8,128)}) %all-gather.111.cloned.1.call-update) | async-done | bytes 1048592 | tf_op jit(solution)/shard_map/all_gather | solution.py:59
  1337.2 16.1 %all-gather.113.cloned.1.call-done = f32[256,1024]{0,1:T(8,128)} async-done(((f32[256,256]{0,1:T(8,128)}), f32[256,1024]{0,1:T(8,128)}) %all-gather.113.cloned.1.call-update) | async-done | bytes 1048592 | tf_op jit(solution)/shard_map/all_gather | solution.py:45
  1360.7 41.5 %all-gather.115.cloned.1.call-done = f32[1024,256]{0,1:T(8,128)} async-done(((f32[256,256]{0,1:T(8,128)}), f32[1024,256]{0,1:T(8,128)}) %all-gather.115.cloned.1.call-update) | async-done | bytes 1048592 | tf_op jit(solution)/shard_map/all_gather | solution.py:47
  1407.7 26.1 %all-gather.117.cloned.1.call-done = f32[1024,256]{1,0:T(8,128)} async-done(((f32[256,256]{1,0:T(8,128)}), f32[1024,256]{1,0:T(8,128)}) %all-gather.117.cloned.1.call-update) | async-done | bytes 1048592 | tf_op jit(solution)/shard_map/all_gather | solution.py:55
  1439.4 14.5 all-gather.119.cloned.1.call-done
  1457.3 16.2 %all_gather.167 = bf16[1024,256]{0,1:T(8,128)(2,1)S(1)} all-gather(bf16[256,256]{0,1:T(8,128)(2,1)S(1)} %get-tuple-element.13), channel_id=1, replica_groups=mesh['groups'=2,'dp'=4,'mp'=4] {'dp'}, dimensions={0}, use_global_device_ids=true | all-gather | bytes 655360 | tf_op jit(solution)/shard_map/all_gather | solution.py:64
  (226 shorter events, 277.7 us)
Async XLA Ops:
  7.2 45.8 %all-reduce.4.cloned.1.call-start = ((), (), s32[]{:S(2)}) async-start(), calls=%async_computation.12 | async-start | bytes 524288 | tf_op jit(solution)/shard_map/psum | solution.py:34
  14.7 72.6 %reduce-scatter.3.cloned.1.call-start = ((), (), s32[]{:S(2)}) async-start(), calls=%async_computation.13 | async-start | bytes 1310720 | tf_op jit(solution)/shard_map/reduce_scatter | solution.py:41
  60.2 76.3 %all-gather.41.cloned.1.call-start = ((), (), s32[]{:S(2)}) async-start(), calls=%async_computation.14 | async-start | bytes 1310720 | tf_op jit(solution)/shard_map/all_gather | solution.py:45
  122.4 63.0 %all-gather.43.cloned.1.call-start = ((), (), s32[]{:S(2)}) async-start(), calls=%async_computation.15 | async-start | bytes 1310720 | tf_op jit(solution)/shard_map/all_gather | solution.py:47
  139.1 47.7 %all-to-all-start = ((f32[256,4,256]{2,0,1:T(8,128)}), f32[256,4,256]{2,0,1:T(8,128)S(1)}, u32[]{:S(2)}, u32[]{:S(2)}) async-start(f32[256,4,256]{2,0,1:T(8,128)} %copy.28), calls=%async_computation.1 | async-start | bytes 2097152 | tf_op jit(solution)/shard_map/all_to_all | solution.py:46
  143.8 73.1 %all-gather.45.cloned.1.call-start = ((), (), s32[]{:S(2)}) async-start(), calls=%async_computation.16 | async-start | bytes 1310720 | tf_op jit(solution)/shard_map/all_gather | solution.py:55
  190.6 46.5 %all-gather.47.cloned.1.call-start = ((), (), s32[]{:S(2)}) async-start(), calls=%async_computation.17 | async-start | bytes 1310720 | tf_op jit(solution)/shard_map/all_gather | solution.py:59
  241.1 65.8 %all-gather.51.cloned.1.call-start = ((), (), s32[]{:S(2)}) async-start(), calls=%async_computation.19 | async-start | bytes 1310720 | tf_op jit(solution)/shard_map/all_gather | solution.py:47
  260.6 47.7 %all-to-all-start.1 = ((f32[256,4,256]{2,0,1:T(8,128)}), f32[256,4,256]{2,0,1:T(8,128)S(1)}, u32[]{:S(2)}, u32[]{:S(2)}) async-start(f32[256,4,256]{2,0,1:T(8,128)} %copy.31), calls=%async_computation.2 | async-start | bytes 2097152 | tf_op jit(solution)/shard_map/all_to_all | solution.py:46
  265.4 73.2 %all-gather.53.cloned.1.call-start = ((), (), s32[]{:S(2)}) async-start(), calls=%async_computation.20 | async-start | bytes 1310720 | tf_op jit(solution)/shard_map/all_gather | solution.py:55
  312.1 46.6 %all-gather.55.cloned.1.call-start = ((), (), s32[]{:S(2)}) async-start(), calls=%async_computation.21 | async-start | bytes 1310720 | tf_op jit(solution)/shard_map/all_gather | solution.py:59
  362.7 65.8 %all-gather.59.cloned.1.call-start = ((), (), s32[]{:S(2)}) async-start(), calls=%async_computation.23 | async-start | bytes 1310720 | tf_op jit(solution)/shard_map/all_gather | solution.py:47
  382.3 47.7 %all-to-all-start.2 = ((f32[256,4,256]{2,0,1:T(8,128)}), f32[256,4,256]{2,0,1:T(8,128)S(1)}, u32[]{:S(2)}, u32[]{:S(2)}) async-start(f32[256,4,256]{2,0,1:T(8,128)} %copy.34), calls=%async_computation.3 | async-start | bytes 2097152 | tf_op jit(solution)/shard_map/all_to_all | solution.py:46
  387.0 73.1 %all-gather.61.cloned.1.call-start = ((), (), s32[]{:S(2)}) async-start(), calls=%async_computation.24 | async-start | bytes 1310720 | tf_op jit(solution)/shard_map/all_gather | solution.py:55
  433.7 46.5 %all-gather.63.cloned.1.call-start = ((), (), s32[]{:S(2)}) async-start(), calls=%async_computation.25 | async-start | bytes 1310720 | tf_op jit(solution)/shard_map/all_gather | solution.py:59
  484.3 65.8 %all-gather.67.cloned.1.call-start = ((), (), s32[]{:S(2)}) async-start(), calls=%async_computation.27 | async-start | bytes 1310720 | tf_op jit(solution)/shard_map/all_gather | solution.py:47
  503.8 47.7 %all-to-all-start.3 = ((f32[256,4,256]{2,0,1:T(8,128)}), f32[256,4,256]{2,0,1:T(8,128)S(1)}, u32[]{:S(2)}, u32[]{:S(2)}) async-start(f32[256,4,256]{2,0,1:T(8,128)} %copy.37), calls=%async_computation.4 | async-start | bytes 2097152 | tf_op jit(solution)/shard_map/all_to_all | solution.py:46
  508.5 73.1 %all-gather.69.cloned.1.call-start = ((), (), s32[]{:S(2)}) async-start(), calls=%async_computation.28 | async-start | bytes 1310720 | tf_op jit(solution)/shard_map/all_gather | solution.py:55
  555.3 46.5 %all-gather.71.cloned.1.call-start = ((), (), s32[]{:S(2)}) async-start(), calls=%async_computation.29 | async-start | bytes 1310720 | tf_op jit(solution)/shard_map/all_gather | solution.py:59
  585.4 37.3 %all-gather.73.cloned.1.call-start = ((), (), s32[]{:S(2)}) async-start(), calls=%async_computation.30 | async-start | bytes 1310720 | tf_op jit(solution)/shard_map/all_gather | solution.py:45
  605.8 65.8 %all-gather.75.cloned.1.call-start = ((), (), s32[]{:S(2)}) async-start(), calls=%async_computation.31 | async-start | bytes 1310720 | tf_op jit(solution)/shard_map/all_gather | solution.py:47
  625.3 47.7 %all-to-all-start.4 = ((f32[256,4,256]{2,0,1:T(8,128)}), f32[256,4,256]{2,0,1:T(8,128)S(1)}, u32[]{:S(2)}, u32[]{:S(2)}) async-start(f32[256,4,256]{2,0,1:T(8,128)} %copy.40), calls=%async_computation.5 | async-start | bytes 2097152 | tf_op jit(solution)/shard_map/all_to_all | solution.py:46
  630.1 73.1 %all-gather.77.cloned.1.call-start = ((), (), s32[]{:S(2)}) async-start(), calls=%async_computation.32 | async-start | bytes 1310720 | tf_op jit(solution)/shard_map/all_gather | solution.py:55
  676.8 46.5 %all-gather.79.cloned.1.call-start = ((), (), s32[]{:S(2)}) async-start(), calls=%async_computation.33 | async-start | bytes 1310720 | tf_op jit(solution)/shard_map/all_gather | solution.py:59
  706.9 78.1 %all-reduce.6.cloned.1.call-start = ((), (), s32[]{:S(2)}) async-start(), calls=%async_computation.34 | async-start | bytes 524288 | tf_op jit(solution)/shard_map/psum | solution.py:34
  749.1 68.6 %reduce-scatter.5.cloned.1.call-start = ((), (), s32[]{:S(2)}) async-start(), calls=%async_computation.35 | async-start | bytes 1310720 | tf_op jit(solution)/shard_map/reduce_scatter | solution.py:41
  790.7 76.3 %all-gather.81.cloned.1.call-start = ((), (), s32[]{:S(2)}) async-start(), calls=%async_computation.36 | async-start | bytes 1310720 | tf_op jit(solution)/shard_map/all_gather | solution.py:45
  852.9 63.0 %all-gather.83.cloned.1.call-start = ((), (), s32[]{:S(2)}) async-start(), calls=%async_computation.37 | async-start | bytes 1310720 | tf_op jit(solution)/shard_map/all_gather | solution.py:47
  869.6 47.7 %all-to-all-start.5 = ((f32[256,4,256]{2,0,1:T(8,128)}), f32[256,4,256]{2,0,1:T(8,128)S(1)}, u32[]{:S(2)}, u32[]{:S(2)}) async-start(f32[256,4,256]{2,0,1:T(8,128)} %copy.42), calls=%async_computation.7 | async-start | bytes 2097152 | tf_op jit(solution)/shard_map/all_to_all | solution.py:46
  874.3 73.1 %all-gather.85.cloned.1.call-start = ((), (), s32[]{:S(2)}) async-start(), calls=%async_computation.38 | async-start | bytes 1310720 | tf_op jit(solution)/shard_map/all_gather | solution.py:55
  921.1 46.5 %all-gather.87.cloned.1.call-start = ((), (), s32[]{:S(2)}) async-start(), calls=%async_computation.39 | async-start | bytes 1310720 | tf_op jit(solution)/shard_map/all_gather | solution.py:59
  971.6 65.8 %all-gather.91.cloned.1.call-start = ((), (), s32[]{:S(2)}) async-start(), calls=%async_computation.41 | async-start | bytes 1310720 | tf_op jit(solution)/shard_map/all_gather | solution.py:47
  991.2 47.7 %all-to-all-start.6 = ((f32[256,4,256]{2,0,1:T(8,128)}), f32[256,4,256]{2,0,1:T(8,128)S(1)}, u32[]{:S(2)}, u32[]{:S(2)}) async-start(f32[256,4,256]{2,0,1:T(8,128)} %copy.45), calls=%async_computation.8 | async-start | bytes 2097152 | tf_op jit(solution)/shard_map/all_to_all | solution.py:46
  995.9 73.1 %all-gather.93.cloned.1.call-start = ((), (), s32[]{:S(2)}) async-start(), calls=%async_computation.42 | async-start | bytes 1310720 | tf_op jit(solution)/shard_map/all_gather | solution.py:55
  1042.6 46.5 %all-gather.95.cloned.1.call-start = ((), (), s32[]{:S(2)}) async-start(), calls=%async_computation.43 | async-start | bytes 1310720 | tf_op jit(solution)/shard_map/all_gather | solution.py:59
  1093.2 65.8 %all-gather.99.cloned.1.call-start = ((), (), s32[]{:S(2)}) async-start(), calls=%async_computation.45 | async-start | bytes 1310720 | tf_op jit(solution)/shard_map/all_gather | solution.py:47
  1112.7 47.7 %all-to-all-start.7 = ((f32[256,4,256]{2,0,1:T(8,128)}), f32[256,4,256]{2,0,1:T(8,128)S(1)}, u32[]{:S(2)}, u32[]{:S(2)}) async-start(f32[256,4,256]{2,0,1:T(8,128)} %copy.48), calls=%async_computation.9 | async-start | bytes 2097152 | tf_op jit(solution)/shard_map/all_to_all | solution.py:46
  1117.4 73.2 %all-gather.101.cloned.1.call-start = ((), (), s32[]{:S(2)}) async-start(), calls=%async_computation.46 | async-start | bytes 1310720 | tf_op jit(solution)/shard_map/all_gather | solution.py:55
  1164.2 46.6 %all-gather.103.cloned.1.call-start = ((), (), s32[]{:S(2)}) async-start(), calls=%async_computation.47 | async-start | bytes 1310720 | tf_op jit(solution)/shard_map/all_gather | solution.py:59
  1214.8 65.8 %all-gather.107.cloned.1.call-start = ((), (), s32[]{:S(2)}) async-start(), calls=%async_computation.49 | async-start | bytes 1310720 | tf_op jit(solution)/shard_map/all_gather | solution.py:47
  1234.3 47.7 %all-to-all-start.8 = ((f32[256,4,256]{2,0,1:T(8,128)}), f32[256,4,256]{2,0,1:T(8,128)S(1)}, u32[]{:S(2)}, u32[]{:S(2)}) async-start(f32[256,4,256]{2,0,1:T(8,128)} %copy.51), calls=%async_computation.10 | async-start | bytes 2097152 | tf_op jit(solution)/shard_map/all_to_all | solution.py:46
  1239.0 73.2 %all-gather.109.cloned.1.call-start = ((), (), s32[]{:S(2)}) async-start(), calls=%async_computation.50 | async-start | bytes 1310720 | tf_op jit(solution)/shard_map/all_gather | solution.py:55
  1285.8 46.6 %all-gather.111.cloned.1.call-start = ((), (), s32[]{:S(2)}) async-start(), calls=%async_computation.51 | async-start | bytes 1310720 | tf_op jit(solution)/shard_map/all_gather | solution.py:59
  1316.0 37.3 %all-gather.113.cloned.1.call-start = ((), (), s32[]{:S(2)}) async-start(), calls=%async_computation.52 | async-start | bytes 1310720 | tf_op jit(solution)/shard_map/all_gather | solution.py:45
  1336.4 65.8 %all-gather.115.cloned.1.call-start = ((), (), s32[]{:S(2)}) async-start(), calls=%async_computation.53 | async-start | bytes 1310720 | tf_op jit(solution)/shard_map/all_gather | solution.py:47
  1355.9 47.7 %all-to-all-start.9 = ((f32[256,4,256]{2,0,1:T(8,128)}), f32[256,4,256]{2,0,1:T(8,128)S(1)}, u32[]{:S(2)}, u32[]{:S(2)}) async-start(f32[256,4,256]{2,0,1:T(8,128)} %copy.54), calls=%async_computation.11 | async-start | bytes 2097152 | tf_op jit(solution)/shard_map/all_to_all | solution.py:46
  1360.7 73.2 %all-gather.117.cloned.1.call-start = ((), (), s32[]{:S(2)}) async-start(), calls=%async_computation.54 | async-start | bytes 1310720 | tf_op jit(solution)/shard_map/all_gather | solution.py:55
  1407.4 46.6 %all-gather.119.cloned.1.call-start = ((), (), s32[]{:S(2)}) async-start(), calls=%async_computation.55 | async-start | bytes 1310720 | tf_op jit(solution)/shard_map/all_gather | solution.py:59
  (29 other events, 2034.9 us)
Sparse Core Ops, SparseCore 0:
  14.8 38.1 all-reduce.3
  60.3 26.8 reduce-scatter.2
  122.5 13.9 all-gather.40
  138.5 46.8 all-gather.42
  190.7 26.1 all-gather.44
  220.8 16.2 all-gather.46
  241.3 16.7 all-gather.48
  260.2 46.7 all-gather.50
  312.2 26.2 all-gather.52
  342.4 16.2 all-gather.54
  362.9 16.7 all-gather.56
  381.6 46.8 all-gather.58
  433.9 26.1 all-gather.60
  464.0 16.2 all-gather.62
  484.4 16.7 all-gather.64
  503.2 46.8 all-gather.66
  555.4 26.1 all-gather.68
  585.5 16.2 all-gather.70
  606.0 16.7 all-gather.72
  624.7 46.8 all-gather.74
  676.9 26.1 all-gather.76
  707.1 16.2 all-gather.78
  749.3 35.7 all-reduce.5
  790.8 26.8 reduce-scatter.4
  853.0 13.9 all-gather.80
  869.0 46.8 all-gather.82
  921.2 26.1 all-gather.84
  951.3 16.2 all-gather.86
  971.8 16.7 all-gather.88
  990.5 46.8 all-gather.90
  1042.7 26.1 all-gather.92
  1072.9 16.2 all-gather.94
  1093.3 16.7 all-gather.96
  1112.2 46.6 all-gather.98
  1164.3 26.2 all-gather.100
  1194.5 16.2 all-gather.102
  1214.9 16.7 all-gather.104
  1233.8 46.7 all-gather.106
  1285.9 26.2 all-gather.108
  1316.1 16.2 all-gather.110
  1336.5 16.7 all-gather.112
  1355.4 46.6 all-gather.114
  1407.5 26.2 all-gather.116
  1437.7 16.2 all-gather.118
where the time goes:
time: 1500 us; the launch traced here: 1490 us
  waiting for transfers between devices  1120 us (75%)
  matrix products  142 us (9%)
  blocking collectives  108 us (7%)
  starting transfers between devices  50 us (3%)
  local copies, waits for them, and re-layouts  41 us (3%)
  between operations  16.4 us (1%)
    all_gather x10, waiting for transfers between devices, body(): col_block = lax.all_gather(polar, 'dp', axis=0, tiled=True)  415 us
    all_gather x10, waiting for transfers between devices, body(): gram_cols = lax.all_gather(gram_piece, 'dp', axis=0, tiled=True)  263 us
    all_gather x10, waiting for transfers between devices, body(): polar_band = lax.all_gather(polar, 'mp', axis=1, tiled=True)  157 us
    all_gather x10, waiting for transfers between devices, body(): first_band = lax.all_gather(first_prod, 'mp', axis=1, tiled=True)  151 us
    psum x2, blocking collectives, body(): square_sum = lax.psum(jnp.sum(cross_tile * cross_tile), ('dp', 'mp'))  62.2 us
    psum x2, waiting for transfers between devices, body(): class_sum, class_count = lax.psum((class_sum, class_count), 'dp')  57.5 us
    reduce_scatter x2, waiting for transfers between devices, body(): lax.psum_scatter(cross_part, 'dp', scatter_dimension=0, tiled=True)  54 us
    all_to_all x10, starting transfers between devices, body(): lax.all_to_all(polar_band, 'dp', split_axis=1, concat_axis=0, tiled=True)  47.3 us
  transfers between devices with their start and end apart: 54, of which 54 were waited for; matrix products, arithmetic and copies ran while one was open for 3% of the time, Pallas kernels for 0%

commit v1 on v0

v1 whole, which is shorter than its diff:
```python
import functools

import jax
import jax.numpy as jnp
from jax import lax
from jax.experimental import pallas as pl
from jax.experimental.pallas import tpu as pltpu
from jax.sharding import PartitionSpec as P

SUB = 64
K = 256
ALTS = 2
NS_STEPS = 5
LOW_STEPS = 2
BLOCK = 512

coef_one = 3.4445
coef_two = -4.775
coef_three = 2.0315

TN = (((0,), (0,)), ((), ()))
NN = (((1,), (0,)), ((), ()))
NT = (((1,), (1,)), ((), ()))


def mul(one, two, dims):
    return lax.dot_general(one, two, dims, preferred_element_type=jnp.float32)


def split(value):
    high = value.astype(jnp.bfloat16)
    low = (value - high.astype(jnp.float32)).astype(jnp.bfloat16)
    return high, low


def mul3(one, two, dims):
    return mul(one[1], two[0], dims) + mul(one[0], two[1], dims) + mul(one[0], two[0], dims)


def polar_kernel(own, cross_ref, out_ref, turn_high, turn_low, gram_high, gram_low, ser_high, ser_low):
    width = cross_ref.shape[0]
    halves = width // BLOCK
    total = jnp.sum(cross_ref[...] * cross_ref[...])
    scale = 1.0 / (jnp.sqrt(jnp.full((1, 1), total, jnp.float32)) + 1e-06)

    def at(tile):
        row = pl.ds(pl.multiple_of((tile // halves) * BLOCK, BLOCK), BLOCK)
        col = pl.ds(pl.multiple_of((tile % halves) * BLOCK, BLOCK), BLOCK)
        return row, col

    def put(high_ref, low_ref, lead, value):
        high, low = split(value)
        high_ref[lead] = high
        if low_ref is not None:
            low_ref[lead] = low

    @pl.loop(0, halves * halves)
    def _(tile):
        row, col = at(tile)
        high, low = split(cross_ref[row, col] * scale)
        turn_high[0, row, col] = high
        turn_low[0, row, col] = low

    for iterate in range(NS_STEPS - 1):
        now, later = iterate % 2, (iterate + 1) % 2
        fine = iterate >= LOW_STEPS

        @pl.loop(0, halves * halves)
        def _(tile):
            row, col = at(tile)
            if fine:
                gram = mul3(
                    (turn_high[now, row, :], turn_low[now, row, :]),
                    (turn_high[now, col, :], turn_low[now, col, :]),
                    NT,
                )
                gram_high[row, col], gram_low[row, col] = split(gram)
            else:
                gram = mul(turn_high[now, row, :], turn_high[now, col, :], NT)
                gram_high[row, col] = gram.astype(jnp.bfloat16)

        @pl.loop(0, halves * halves)
        def _(tile):
            row, col = at(tile)
            if fine:
                square = mul3(
                    (gram_high[row, :], gram_low[row, :]), (gram_high[:, col], gram_low[:, col]), NN
                )
                gram = gram_high[row, col].astype(jnp.float32) + gram_low[row, col].astype(jnp.float32)
                series = coef_two * gram + coef_three * square
                ser_high[row, col], ser_low[row, col] = split(series)
            else:
                square = mul(gram_high[row, :], gram_high[:, col], NN)
                gram = gram_high[row, col].astype(jnp.float32)
                ser_high[row, col] = (coef_two * gram + coef_three * square).astype(jnp.bfloat16)

        @pl.loop(0, halves * halves)
        def _(tile):
            row, col = at(tile)
            turn = turn_high[now, row, col].astype(jnp.float32) + turn_low[now, row, col].astype(
                jnp.float32
            )
            if fine:
                step = mul3(
                    (ser_high[row, :], ser_low[row, :]),
                    (turn_high[now, :, col], turn_low[now, :, col]),
                    NN,
                )
            else:
                step = mul(ser_high[row, :], turn_high[now, :, col], NN)
            high, low = split(coef_one * turn + step)
            turn_high[later, row, col] = high
            turn_low[later, row, col] = low

    now = (NS_STEPS - 1) % 2
    mine = pl.ds(pl.multiple_of(lax.axis_index("mp") * own, own), own)
    whole = (turn_high.at[now], turn_low.at[now])
    base = (whole[0][mine, :], whole[1][mine, :])

    def by_blocks(left, dims):
        parts = []
        for start in range(0, width, BLOCK):
            part = slice(start, start + BLOCK)
            if dims is NT:
                right = (whole[0][part, :], whole[1][part, :])
            else:
                right = (whole[0][:, part], whole[1][:, part])
            parts.append(mul3(left, right, dims))
        return jnp.concatenate(parts, axis=1)

    gram = by_blocks(base, NT)
    first = by_blocks(split(gram), NN)
    square = by_blocks(split(first), NT)
    series = coef_two * gram + coef_three * square
    step = by_blocks(split(series), NN)
    turn = base[0].astype(jnp.float32) + base[1].astype(jnp.float32)
    out_ref[...] = coef_one * turn + step


def polar_rows(cross, own):
    width = cross.shape[0]
    square = (width, width)
    return pl.pallas_call(
        functools.partial(polar_kernel, own),
        out_shape=jax.ShapeDtypeStruct((own, width), jnp.float32),
        in_specs=[pl.BlockSpec(memory_space=pltpu.VMEM)],
        out_specs=pl.BlockSpec(memory_space=pltpu.VMEM),
        scratch_shapes=[
            pltpu.VMEM((2,) + square, jnp.bfloat16),
            pltpu.VMEM((2,) + square, jnp.bfloat16),
            pltpu.VMEM(square, jnp.bfloat16),
            pltpu.VMEM(square, jnp.bfloat16),
            pltpu.VMEM(square, jnp.bfloat16),
            pltpu.VMEM(square, jnp.bfloat16),
        ],
        compiler_params=pltpu.CompilerParams(vmem_limit_bytes=48 * 1024 * 1024),
        cost_estimate=pl.CostEstimate(
            flops=60 * width * width * width, bytes_accessed=8 * width * width, transcendentals=0
        ),
        name="polar_steps",
    )(cross)


def body(embeddings, rotation, codes):
    col_count = rotation.shape[1]
    width = rotation.shape[0]
    local_subs = col_count // SUB
    row_count = embeddings.shape[0]
    levels = jnp.arange(K, dtype=jnp.int32)
    dp_at = lax.axis_index("dp")
    tile_rows = width // lax.axis_size("dp")
    turn_rows = None
    for alternation in range(ALTS):
        if alternation == 0:
            turned = mul(embeddings, rotation, NN).astype(jnp.bfloat16)
        else:
            turned = mul(embeddings, turn_rows.astype(jnp.bfloat16), NT).astype(jnp.bfloat16)
        selector = (codes[alternation][:, :, None] == levels).astype(jnp.bfloat16)
        pieces = turned.reshape(row_count, local_subs, SUB)
        class_sum = jnp.einsum("rlk,rls->kls", selector, pieces, preferred_element_type=jnp.float32)
        class_count = jnp.sum(selector, axis=0, dtype=jnp.float32).T
        class_sum, class_count = lax.psum((class_sum, class_count), "dp")
        centres = (class_sum / (class_count[:, :, None] + 1.0)).astype(jnp.bfloat16)
        picked = jnp.einsum("rlk,kls->rls", selector, centres, preferred_element_type=jnp.float32)
        picked = picked.astype(jnp.bfloat16).reshape(row_count, col_count)
        cross_part = mul(picked, embeddings, TN)
        cross_tile = lax.psum_scatter(cross_part, "dp", scatter_dimension=0, tiled=True)
        cross = lax.all_gather(cross_tile, ("mp", "dp"), axis=0, tiled=True)
        turn_rows = polar_rows(cross, col_count)
    rotated = mul(embeddings, turn_rows.astype(jnp.bfloat16), NT).astype(jnp.bfloat16)
    polar_tile = lax.dynamic_slice_in_dim(turn_rows, dp_at * tile_rows, tile_rows, 1).T
    return (centres.reshape(K, col_count), polar_tile, rotated)


def solution(mesh):
    placed = (P(("groups", "dp"), None), P(None, "mp"), P(None, ("groups", "dp"), "mp"))
    return jax.shard_map(
        body,
        mesh=mesh,
        in_specs=placed,
        out_specs=(P("groups", "mp"), P(("groups", "dp"), "mp"), P(("groups", "dp"), "mp")),
        check_vma=False,
    )
```

time: 1500 us -> 427 us (0.28)
  waiting for transfers between devices: 1120 us -> 212 us
  Pallas kernels: 0 us -> 147 us
  matrix products: 142 us -> 23.6 us
  blocking collectives: 108 us -> 13.7 us
  starting transfers between devices: 50 us -> 0.24 us
  local copies, waits for them, and re-layouts: 41 us -> 8.33 us
    all_gather x40 -> x2, waiting for transfers between devices: 986 us -> 102 us  [body(): cross = lax.all_gather(cross_tile, ('mp', 'dp'), axis=0, tiled=True)]
    pallas_call x0 -> x2, Pallas kernels: none -> 147 us  [polar_rows(): pl.pallas_call(functools.partial(polar_kernel, own), out_shape=jax.ShapeD...]
    dot_general x35 -> x5, matrix products: 131 us -> 12.7 us  [mul(): return lax.dot_general(one, two, dims, preferred_element_type=jnp.float32)]
    psum x2 -> x0, blocking collectives: 62.2 us -> none  [body(): square_sum = lax.psum(jnp.sum(cross_tile * cross_tile), ('dp', 'mp'))]
    all_to_all x10 -> x0, starting transfers between devices: 47.3 us -> none  [body(): lax.all_to_all(polar_band, 'dp', split_axis=1, concat_axis=0, tiled=True)]
    all_gather x2 -> x0, blocking collectives: 32.3 us -> none  [body(): lax.all_gather(polar.astype(jnp.bfloat16), 'dp', axis=0, tiled=True)]
    all_to_all x10 -> x0, local copies, waits for them, and re-layouts: 26.2 us -> none  [body(): lax.all_to_all(polar_band, 'dp', split_axis=1, concat_axis=0, tiled=True)]
  transfers between devices with their start and end apart: 54 -> 6, of which waited for: 54 -> 6; matrix products, arithmetic and copies ran while one was open for 3% -> 1% of each run, Pallas kernels for 0% -> 0%
where the time goes in v1:
time: 427 us; the launch traced here: 423 us
  waiting for transfers between devices  212 us (50%)
  Pallas kernels  147 us (34%)
  matrix products  23.6 us (6%)
  between operations  14.4 us (3%)
  blocking collectives  13.7 us (3%)
  local copies, waits for them, and re-layouts  8.33 us (2%)
    pallas_call x2, Pallas kernels, polar_rows(): pl.pallas_call(functools.partial(polar_kernel, own), out_shape=jax.ShapeD...  147 us
    all_gather x2, waiting for transfers between devices, body(): cross = lax.all_gather(cross_tile, ('mp', 'dp'), axis=0, tiled=True)  102 us
    psum x2, waiting for transfers between devices, body(): class_sum, class_count = lax.psum((class_sum, class_count), 'dp')  55.6 us
    reduce_scatter x2, waiting for transfers between devices, body(): lax.psum_scatter(cross_part, 'dp', scatter_dimension=0, tiled=True)  54 us
    psum x1, blocking collectives, body(): class_sum, class_count = lax.psum((class_sum, class_count), 'dp')  13.7 us
    dot_general x5, matrix products, mul(): return lax.dot_general(one, two, dims, preferred_element_type=jnp.float32)  12.7 us
  transfers between devices with their start and end apart: 6, of which 6 were waited for; matrix products, arithmetic and copies ran while one was open for 1% of the time, Pallas kernels for 0%

profile of v1, /device:TPU:0, one launch (start us, length us, event | category | flops | bytes accessed | tf_op | source)
XLA Modules:
  0.0 422.7 jit_solution(13062346014222687791)
XLA Ops:
  7.2 0.0 copy-start
  7.2 0.0 all-reduce.4.cloned.1.call-start
  7.2 0.8 slice_bitcast_fusion
  8.1 0.2 copy-done
  8.2 3.5 convolution_convert_fusion.2
  11.7 2.9 fusion.13
  14.6 0.0 all-reduce.4.cloned.1.call-update
  14.7 0.0 reduce-scatter.3.cloned.1.call-start
  14.7 2.9 convert_reduce_fusion
  17.6 13.7 %all-reduce = (f32[256,4]{0,1:T(4,128)S(1)}, f32[256,4]{0,1:T(4,128)S(1)}) all-reduce(f32[256,4]{0,1:T(4,128)S(1)} %bitcast.38, f32[256,4]{0,1:T(4,128)S(1)} %bitcast.37), channel_id=1, replica_groups=mesh['groups'=2,'dp'=4,'mp'=4] {'dp'}, use_global_device_ids=true, to_apply=%region_2.0 | all-reduce | flops 2048 | bytes 16384 | tf_op jit(solution)/shard_map/psum | solution.py:182
  31.3 21.7 %all-reduce.4.cloned.1.call-done = f32[256,4,64]{0,2,1:T(8,128)} async-done(((f32[256,4,64]{0,2,1:T(8,128)}), f32[256,4,64]{0,2,1:T(8,128)}) %all-reduce.4.cloned.1.call-update) | async-done | bytes 262160 | tf_op jit(solution)/shard_map/psum | solution.py:182
  52.9 2.8 fusion.10
  55.8 4.4 %fusion.18 = f32[256,1024]{1,0:T(8,128)} fusion(bf16[2048,256]{0,1:T(8,128)(2,1)S(1)} %bitcast.39, bf16[2048,1024]{1,0:T(8,128)(2,1)} %param.3), kind=kOutput, calls=%fused_computation.32 | convolution fusion | flops 1073741824 | bytes 6291456 | tf_op jit(solution)/shard_map/dot_general | solution.py:27
  60.2 0.0 reduce-scatter.3.cloned.1.call-update
  60.2 0.0 all-gather.3.cloned.1.call-start
  60.3 27.0 %reduce-scatter.3.cloned.1.call-done = f32[64,1024]{1,0:T(8,128)} async-done(((f32[256,1024]{1,0:T(8,128)}), f32[64,1024]{1,0:T(8,128)}) %reduce-scatter.3.cloned.1.call-update) | async-done | bytes 262160 | tf_op jit(solution)/shard_map/reduce_scatter | solution.py:187
  87.3 0.0 all-gather.3.cloned.1.call-update
  87.3 0.0 all-reduce.6.cloned.1.call-start
  87.3 51.5 %all-gather.3.cloned.1.call-done.cross_ref = f32[1024,1024]{1,0:T(8,128)} async-done(((f32[64,1024]{1,0:T(8,128)}), f32[1024,1024]{1,0:T(8,128)}) %all-gather.3.cloned.1.call-update) | async-done | bytes 4194320 | tf_op jit(solution)/shard_map/all_gather | solution.py:188
  138.9 0.0 copy-start.2
  138.9 2.2 copy-done.2
  141.1 0.0 copy-start.3
  141.1 73.2 %polar_steps.2 = f32[256,1024]{1,0:T(8,128)S(1)} custom-call(f32[1024,1024]{1,0:T(8,128)S(1)} %copy-done.2), custom_call_target="tpu_custom_call" | custom-call | flops 64424509440 | bytes 8388608 | tf_op jit(solution)/shard_map/polar_steps/pallas_call | solution.py:143
  214.2 0.0 copy-done.3
  214.2 1.3 convolution_convert_fusion.1
  215.5 2.9 fusion.14
  218.4 0.0 all-reduce.6.cloned.1.call-update
  218.5 0.0 reduce-scatter.5.cloned.1.call-start
  218.5 33.9 %all-reduce.6.cloned.1.call-done = f32[256,4,64]{0,2,1:T(8,128)} async-done(((f32[256,4,64]{0,2,1:T(8,128)}), f32[256,4,64]{0,2,1:T(8,128)}) %all-reduce.6.cloned.1.call-update) | async-done | bytes 262160 | tf_op jit(solution)/shard_map/psum | solution.py:182
  252.5 0.0 copy-start.4
  252.5 1.1 divide_convert_fusion
  253.6 2.2 fusion.11
  255.8 0.0 copy-done.4
  255.9 2.2 fusion.19
  258.1 0.0 reduce-scatter.5.cloned.1.call-update
  258.1 0.0 all-gather.5.cloned.1.call-start
  258.2 27.0 %reduce-scatter.5.cloned.1.call-done = f32[64,1024]{1,0:T(8,128)} async-done(((f32[256,1024]{1,0:T(8,128)}), f32[64,1024]{1,0:T(8,128)}) %reduce-scatter.5.cloned.1.call-update) | async-done | bytes 262160 | tf_op jit(solution)/shard_map/reduce_scatter | solution.py:187
  285.2 0.0 all-gather.5.cloned.1.call-update
  285.2 0.8 copy.6
  286.0 50.7 %all-gather.5.cloned.1.call-done.cross_ref = f32[1024,1024]{1,0:T(8,128)} async-done(((f32[64,1024]{1,0:T(8,128)}), f32[1024,1024]{1,0:T(8,128)}) %all-gather.5.cloned.1.call-update) | async-done | bytes 4194320 | tf_op jit(solution)/shard_map/all_gather | solution.py:188
  336.6 0.0 copy-start.1
  336.6 2.2 copy-done.1
  338.8 0.0 copy-start.5
  338.8 73.4 %polar_steps.3 = f32[256,1024]{1,0:T(8,128)S(1)} custom-call(f32[1024,1024]{1,0:T(8,128)S(1)} %copy-done.1), custom_call_target="tpu_custom_call" | custom-call | flops 64424509440 | bytes 8388608 | tf_op jit(solution)/shard_map/polar_steps/pallas_call | solution.py:143
  412.2 0.0 copy-done.5
  412.2 1.3 fusion.12
  413.5 0.8 copy.7
  414.4 1.3 copy.8
  (3 shorter events, 0.0 us)
Async XLA Ops:
  7.2 1.1 copy-start
  7.2 45.8 %all-reduce.4.cloned.1.call-start = ((), (), s32[]{:S(2)}) async-start(), calls=%async_computation.2 | async-start | bytes 524288 | tf_op jit(solution)/shard_map/psum | solution.py:182
  14.7 72.6 %reduce-scatter.3.cloned.1.call-start = ((), (), s32[]{:S(2)}) async-start(), calls=%async_computation.3 | async-start | bytes 1310720 | tf_op jit(solution)/shard_map/reduce_scatter | solution.py:187
  60.2 78.6 %all-gather.3.cloned.1.call-start = ((), (), s32[]{:S(2)}) async-start(), calls=%async_computation.4 | async-start | bytes 4456448 | tf_op jit(solution)/shard_map/all_gather | solution.py:188
  87.3 165.2 %all-reduce.6.cloned.1.call-start = ((), (), s32[]{:S(2)}) async-start(), calls=%async_computation.5 | async-start | bytes 524288 | tf_op jit(solution)/shard_map/psum | solution.py:182
  138.9 2.2 copy-start.2
  141.1 73.2 %copy-start.3 = (bf16[2048,1024]{1,0:T(8,128)(2,1)S(1)}, bf16[2048,1024]{1,0:T(8,128)(2,1)}, u32[]{:S(2)}) copy-start(bf16[2048,1024]{1,0:T(8,128)(2,1)} %param.3) | copy-start | bytes 12582916
  218.5 66.7 %reduce-scatter.5.cloned.1.call-start = ((), (), s32[]{:S(2)}) async-start(), calls=%async_computation.6 | async-start | bytes 1310720 | tf_op jit(solution)/shard_map/reduce_scatter | solution.py:187
  252.5 3.4 copy-start.4
  258.1 78.5 %all-gather.5.cloned.1.call-start = ((), (), s32[]{:S(2)}) async-start(), calls=%async_computation.7 | async-start | bytes 4456448 | tf_op jit(solution)/shard_map/all_gather | solution.py:188
  336.6 2.2 copy-start.1
  338.8 73.4 %copy-start.5 = (bf16[2048,1024]{1,0:T(8,128)(2,1)S(1)}, bf16[2048,1024]{1,0:T(8,128)(2,1)}, u32[]{:S(2)}) copy-start(bf16[2048,1024]{1,0:T(8,128)(2,1)} %param.3) | copy-start | bytes 12582916
Sparse Core Ops, SparseCore 0:
  14.8 38.1 all-reduce.3
  60.4 26.8 reduce-scatter.2
  89.5 49.3 all-gather.2
  218.6 33.8 all-reduce.5
  258.2 26.8 reduce-scatter.4
  287.2 49.3 all-gather.4
